TPU v7x, 256 devices: a whole 4x4x8 slice. The times are simulated.
256 devices in a mesh: row: 16 (over y, x_hi, core), col: 16 (over x_lo, z).
Axes of the slice: x: 4 (x_hi: 2, x_lo: 2; x = x_hi * 2 + x_lo), y: 4, z: 8, core: 2. Of those that a mesh axis runs over, the one named last changes fastest.
Arguments:
- inputs: bfloat16 [512, 8192], P('col', 'row'), may hold values from -6 to 6
- out_grad: bfloat16 [512, 8192], P('col', 'row'), may hold values from -6 to 6
- gate_weight: bfloat16 [8192, 29568], P('row', 'col'), may hold values from -0.0625 to 0.0625
- up_weight: bfloat16 [8192, 29568], P('row', 'col'), may hold values from -0.0625 to 0.0625
- down_weight: bfloat16 [29568, 8192], P('col', 'row'), may hold values from -0.03125 to 0.03125
Outputs:
- grad_input: bfloat16 [512, 8192], P('col', 'row')
- grad_gate: bfloat16 [8192, 29568], P('row', 'col')
- grad_up: bfloat16 [8192, 29568], P('row', 'col')
- grad_down: bfloat16 [29568, 8192], P('col', 'row')
All inputs are finite; a program needn't handle non-finite values.
Results may differ from a plain program's by a relative error of at most 0.0049.
Values may be sent and summed in bfloat16 or wider, within the bound.
A program may use at most 128 MiB of HBM per device.

v0:
```python
import jax
import jax.numpy as jnp
from jax import lax
from jax.sharding import PartitionSpec as P


def contract_last(left, right):
    return lax.dot_general(
        left, right, (((1,), (1,)), ((), ())), preferred_element_type=jnp.float32
    )


def contract_first(left, right):
    return lax.dot_general(
        left, right, (((0,), (0,)), ((), ())), preferred_element_type=jnp.float32
    )


def pointwise(gate, up, back):
    sig = jax.nn.sigmoid(gate)
    act = gate * sig
    hidden = (act * up).astype(jnp.bfloat16)
    dgate = (back * up * sig * (1.0 + gate * (1.0 - sig))).astype(jnp.bfloat16)
    dup = (back * act).astype(jnp.bfloat16)
    return (hidden, dgate, dup)


def on_device(inputs, out_grad, gate_weight, up_weight, down_weight):
    inputs_all, grads_all = (
        lax.all_gather(inputs, "col", axis=0, tiled=True),
        lax.all_gather(out_grad, "col", axis=0, tiled=True),
    )
    gate_part = jnp.dot(inputs_all, gate_weight, preferred_element_type=jnp.float32)
    up_part = jnp.dot(inputs_all, up_weight, preferred_element_type=jnp.float32)
    back_part = contract_last(grads_all, down_weight)
    stacked = jnp.stack([gate_part, up_part, back_part])
    summed = lax.psum(stacked, "row")
    hidden, dgate, dup = pointwise(summed[0], summed[1], summed[2])
    grad_down = contract_first(hidden, grads_all).astype(jnp.bfloat16)
    grad_gate = contract_first(inputs_all, dgate).astype(jnp.bfloat16)
    grad_up = contract_first(inputs_all, dup).astype(jnp.bfloat16)
    grad_input = lax.psum_scatter(
        contract_last(dgate, gate_weight) + contract_last(dup, up_weight),
        "col",
        scatter_dimension=0,
        tiled=True,
    ).astype(jnp.bfloat16)
    return (grad_input, grad_gate, grad_up, grad_down)


def solution(mesh):
    placed = (P("col", "row"), P("col", "row"), P("row", "col"), P("row", "col"), P("col", "row"))
    return jax.shard_map(
        on_device,
        mesh=mesh,
        in_specs=placed,
        out_specs=(P("col", "row"), P("row", "col"), P("row", "col"), P("col", "row")),
        check_vma=False,
    )
```

profile of v0, /device:TPU:2, one launch (start us, length us, event | category | flops | bytes accessed | tf_op | source)
XLA Modules:
  0.0 436.4 jit_solution(6287568668302845044)
XLA Ops:
  7.2 0.0 copy-start
  7.2 0.0 all-reduce.2.cloned.1.call-start
  7.2 38.8 %all_gather.6 = bf16[512,512]{1,0:T(8,128)(2,1)S(1)} all-gather(bf16[32,512]{1,0:T(8,128)(2,1)} %param.5), channel_id=1, replica_groups=mesh['row'=16,'col'=16] {'col'}, dimensions={0}, use_global_device_ids=true | all-gather | bytes 557056 | tf_op jit(solution)/shard_map/all_gather | solution.py:30
  46.1 32.9 %all_gather.7 = bf16[512,512]{1,0:T(8,128)(2,1)S(1)} all-gather(bf16[32,512]{1,0:T(8,128)(2,1)} %param.6), channel_id=1, replica_groups=mesh['row'=16,'col'=16] {'col'}, dimensions={0}, use_global_device_ids=true | all-gather | bytes 557056 | tf_op jit(solution)/shard_map/all_gather | solution.py:31
  78.9 2.7 convolution_bitcast_fusion.1
  81.7 0.0 copy-done
  81.7 0.0 copy-start.5
  81.7 1.2 convolution_bitcast_fusion.2
  82.9 0.3 copy-done.5
  83.2 1.2 convolution_bitcast_fusion
  84.4 4.7 %pad_maximum_fusion = f32[3,512,1848]{1,2,0:T(8,128)} fusion(f32[1,512,1848]{1,2,0:T(8,128)S(1)} %convolution_bitcast_fusion, f32[1,512,1848]{1,2,0:T(8,128)S(1)} %convolution_bitcast_fusion.1, f32[1,512,1848]{1,2,0:T(8,128)S(1)} %convolution_bitcast_fusion.2), kind=kLoop, calls=%fused_computation | loop fusion | flops 5677056 | bytes 22708224 | tf_op jit(solution)/shard_map/stack | solution.py:36
  89.0 0.0 all-reduce.2.cloned.1.call-update
  89.1 0.0 reduce-scatter.2.cloned.1.call-start
  89.1 259.2 %all-reduce.2.cloned.1.call-done = f32[3,512,1848]{1,2,0:T(8,128)} async-done(((f32[3,512,1848]{1,2,0:T(8,128)}), f32[3,512,1848]{1,2,0:T(8,128)}) %all-reduce.2.cloned.1.call-update) | async-done | bytes 11354128 | tf_op jit(solution)/shard_map/psum | solution.py:37
  348.3 5.2 %multiply_convert_fusion.1 = (bf16[512,1848]{0,1:T(8,128)(2,1)S(1)}, bf16[512,1848]{0,1:T(8,128)(2,1)S(1)}) fusion(f32[3,512,1848]{1,2,0:T(8,128)} %all-reduce.2.cloned.1.call-done), kind=kLoop, calls=%fused_computation.5 | loop fusion | flops 12300288 | bytes 15138816 | tf_op jit(solution)/shard_map/convert_element_type | solution.py:24
  353.5 0.0 copy-start.4
  353.5 0.0 copy-start.2
  353.5 0.0 copy-start.1
  353.6 1.2 copy-done.4
  354.8 1.3 fusion.5
  356.1 0.0 copy-done.2
  356.1 0.4 copy-done.1
  356.4 2.3 convolution_add_fusion
  358.7 0.0 reduce-scatter.2.cloned.1.call-update
  358.7 0.0 copy-start.3
  358.7 4.1 fusion.1
  362.8 0.0 copy-done.3
  362.8 2.4 fusion.2
  365.2 5.7 %convolution_convert_fusion = bf16[1848,512]{1,0:T(8,128)(2,1)} fusion(bf16[512,512]{1,0:T(8,128)(2,1)S(1)} %all_gather.7, f32[3,512,1848]{1,2,0:T(8,128)} %all-reduce.2.cloned.1.call-done), kind=kOutput, calls=%fused_computation.12 | convolution fusion | flops 975507456 | bytes 9986048 | tf_op jit(solution)/shard_map/dot_general | solution.py:14
  370.9 57.1 %reduce-scatter.2.cloned.1.call-done = f32[32,512]{1,0:T(8,128)} async-done(((f32[512,512]{1,0:T(8,128)}), f32[32,512]{1,0:T(8,128)}) %reduce-scatter.2.cloned.1.call-update) | async-done | bytes 65552 | tf_op jit(solution)/shard_map/reduce_scatter | solution.py:42
  428.1 1.5 convert_element_type.29
Async XLA Ops:
  7.2 74.5 %copy-start = (bf16[512,1848]{0,1:T(8,128)(2,1)S(1)}, bf16[512,1848]{0,1:T(8,128)(2,1)}, u32[]{:S(2)}) copy-start(bf16[512,1848]{0,1:T(8,128)(2,1)} %param.7) | copy-start | bytes 5677060
  7.2 341.2 %all-reduce.2.cloned.1.call-start = ((), (), s32[]{:S(2)}) async-start(), calls=%async_computation.1 | async-start | bytes 22708224 | tf_op jit(solution)/shard_map/psum | solution.py:37
  81.7 1.5 copy-start.5
  89.1 339.0 %reduce-scatter.2.cloned.1.call-start = ((), (), s32[]{:S(2)}) async-start(), calls=%async_computation.2 | async-start | bytes 1114112 | tf_op jit(solution)/shard_map/reduce_scatter | solution.py:42
  353.5 1.2 copy-start.4
  353.5 2.5 copy-start.2
  353.5 2.9 copy-start.1
  358.7 4.1 copy-start.3
Sparse Core Ops, SparseCore 0:
  89.2 259.1 all-reduce.1
  358.9 69.1 reduce-scatter.1
where the time goes:
time: 438 us; the launch traced here: 436 us
  waiting for transfers between devices  316 us (72%)
  blocking collectives  71.7 us (16%)
  matrix products  20.9 us (5%)
  between operations  14.1 us (3%)
  other arithmetic  11.3 us (3%)
    psum x1, waiting for transfers between devices, on_device(): summed = lax.psum(stacked, 'row')  259 us
    reduce_scatter x1, waiting for transfers between devices, on_device(): lax.psum_scatter(contract_last(dgate, gate_weight) + contract_last(dup, u...  57.1 us
    all_gather x1, blocking collectives, on_device(): lax.all_gather(inputs, 'col', axis=0, tiled=True)  38.8 us
    all_gather x1, blocking collectives, on_device(): lax.all_gather(out_grad, 'col', axis=0, tiled=True)  32.9 us
    dot_general x3, matrix products, contract_first(): lax.dot_general(left, right, (((0,), (0,)), ((), ())), preferred_element_...  12.2 us
  transfers between devices with their start and end apart: 2, of which 2 were waited for; matrix products, arithmetic and copies ran while one was open for 3% of the time, Pallas kernels for 0%

commit v1 on v0

v1 whole, which is shorter than its diff:
```python
import functools

import jax
import jax.numpy as jnp
from jax import lax
from jax.experimental import pallas as pl
from jax.experimental.pallas import tpu as pltpu
from jax.sharding import PartitionSpec as P

MESH = pl.DeviceIdType.MESH
F32, BF16 = jnp.float32, jnp.bfloat16

NEAR = [(dz, dx) for dz in (0, 1, -1, 2, -2, 3, -3, 4) for dx in (0, 1)]
OWNERS = [(dy, dh) for dy in (1, 3, 2, 0) for dh in (0, 1) if (dy, dh) != (0, 0)]
CHUNK = 640
UNITS = [(g, k) for g in range(2) for k in range(3)]


def contract(left, right, left_dim, right_dim):
    return lax.dot_general(
        left,
        right,
        (((left_dim,), (right_dim,)), ((), ())),
        preferred_element_type=F32,
    )


def pointwise(gate, up, back):
    sig = jax.nn.sigmoid(gate)
    act = gate * sig
    hidden = act * up
    dgate = back * up * sig * (1.0 + gate * (1.0 - sig))
    dup = back * act
    return hidden.astype(BF16), dgate.astype(BF16), dup.astype(BF16)


def kernel(
    x_in, g_in, wg_in, wu_in, wd_in,
    gi_out, gg_out, gu_out, gd_out,
    wg, wu, wd, x_all, g_all, x_t, part, pair, terms, got, acts, gi_acc, gi_send,
    gi_got, gg, gu, gd, gi,
    w_sem, gx_send, gx_recv, gg_send, gg_recv, pair_send, pair_recv, rs_send, rs_recv,
    ag_send, ag_recv, fw_send, fw_recv, gi_ssem, gi_rsem, out_sem,
):
    row, col = lax.axis_index("row"), lax.axis_index("col")
    y, h, c = row // 4, (row // 2) % 2, row % 2
    xl, z = col // 8, col % 8
    me = row // 2
    ff = wg.shape[1]

    def in_row(dy, dh):
        return ((y + dy) % 4) * 2 + (h + dh) % 2

    def owner_at(dy, dh):
        return {"row": in_row(dy, dh) * 2 + c, "col": col}

    def near_at(dz, dx):
        return {"row": row, "col": ((xl + dx) % 2) * 8 + (z + dz + 8) % 8}

    partner = {"row": me * 2 + 1 - c, "col": col}

    def remote(src, dst, send, recv, to):
        return pltpu.make_async_remote_copy(
            src_ref=src, dst_ref=dst, send_sem=send, recv_sem=recv, device_id=to, device_id_type=MESH
        )

    def width(k):
        return min(CHUNK, ff - k * CHUNK)

    loads = [
        pltpu.make_async_copy(src, dst, w_sem.at[i])
        for i, (src, dst) in enumerate(
            [(x_in, x_all.at[0]), (g_in, g_all.at[0]), (wg_in, wg), (wu_in, wu), (wd_in, wd)]
        )
    ]
    for load in loads:
        load.start()

    barrier = pltpu.get_barrier_semaphore()
    peers = [partner] + [owner_at(*s) for s in OWNERS] + [near_at(*s) for s in NEAR[1:]]
    for peer in peers:
        pl.semaphore_signal(barrier, inc=1, device_id=peer, device_id_type=MESH)
    pl.semaphore_wait(barrier, len(peers))

    gathers = {}
    for first in (0, 8):
        for name, src, dst, send, recv in (
            ("x", x_in, x_all, gx_send, gx_recv),
            ("g", g_in, g_all, gg_send, gg_recv),
        ):
            for i in range(max(first, 1), first + 8):
                dz, dx = NEAR[i]
                copy = remote(src, dst.at[i], send.at[i], recv.at[i], near_at(-dz, dx))
                copy.start()
                gathers[name, i] = copy

    started = list(gathers.values())

    def landed(name, group):
        for i in range(max(group * 8, 1), group * 8 + 8):
            gathers[name, i].wait_recv()
        if group == 0:
            loads[0 if name == "x" else 1].wait()

    def tokens(ref, group):
        return ref[group * 8 : group * 8 + 8].reshape(256, 512)

    pairs, scatters, spreads, forwards = {}, {}, {}, {}

    def multiply(u):
        g, k = UNITS[u]
        w = width(k)
        lanes = slice(k * CHUNK, k * CHUNK + w)
        if w < CHUNK:
            part[u, :, :, :, :, CHUNK - 128 :] = jnp.zeros((3, 2, 8, 16, 128), F32)
        if k == 0:
            landed("x", g)
        if u == 0:
            loads[2].wait()
            loads[3].wait()
        xs = tokens(x_all, g)
        part[u, 0, :, :, :, :w] = contract(xs, wg[:, lanes], 1, 0).reshape(2, 8, 16, w)
        part[u, 1, :, :, :, :w] = contract(xs, wu[:, lanes], 1, 0).reshape(2, 8, 16, w)
        if k == 0:
            landed("g", g)
        if u == 0:
            loads[4].wait()
        part[u, 2, :, :, :, :w] = contract(tokens(g_all, g), wd[lanes, :], 1, 1).reshape(2, 8, 16, w)
        pairs[u] = remote(part.at[u, :, 1 - c], pair.at[u], pair_send.at[u], pair_recv.at[u], partner)
        pairs[u].start()

    def scatter(u):
        pairs[u].wait_recv()
        for a in range(3):
            terms[u, a] = (part[u, a, c] + pair[u, a]).astype(BF16)
        for i, step in enumerate(OWNERS):
            copy = remote(
                terms.at[u, :, in_row(*step)], got.at[u, i], rs_send.at[u, i], rs_recv.at[u, i], owner_at(*step)
            )
            copy.start()
            scatters[u, i] = copy

    def reduce(u):
        for i in range(7):
            scatters[u, i].wait_recv()
        sums = []
        for a in range(3):
            total = part[u, a, c, me] + pair[u, a, me]
            for i in range(7):
                total = total + got[u, i, a].astype(F32)
            sums.append(total)
        for a, value in enumerate(pointwise(*sums)):
            acts[u, a, c, me] = value
        for i, step in enumerate(OWNERS):
            block = acts.at[u, :, c, me]
            copy = remote(block, block, ag_send.at[u, i], ag_recv.at[u, i], owner_at(*step))
            copy.start()
            spreads[u, i] = copy

    def forward(u):
        for i in range(7):
            spreads[u, i].wait_recv()
        half = acts.at[u, :, c]
        copy = remote(half, half, fw_send.at[u], fw_recv.at[u], partner)
        copy.start()
        forwards[u] = copy

    def act(u, a):
        return acts[u, a].reshape(256, CHUNK)[:, : width(UNITS[u][1])]

    gi_copies = {}

    def input_grad(u):
        g, k = UNITS[u]
        lanes = slice(k * CHUNK, k * CHUNK + width(k))
        forwards[u].wait_recv()
        term = contract(act(u, 1), wg[:, lanes], 1, 1) + contract(act(u, 2), wu[:, lanes], 1, 1)
        if k > 0:
            term = term + gi_acc[g]
        gi_acc[g] = term
        if k == 2:
            gi_send[g] = term.astype(BF16).reshape(8, 32, 512)
            for b in range(8):
                i = g * 8 + b
                if i:
                    copy = remote(gi_send.at[g, b], gi_got.at[i], gi_ssem.at[i], gi_rsem.at[i], near_at(*NEAR[i]))
                    copy.start()
                    gi_copies[i] = copy

    def weight_grads(k):
        w = width(k)
        lanes = slice(k * CHUNK, k * CHUNK + w)
        for a, out in ((1, gg), (2, gu)):
            total = contract(x_t[:, :256], act(k, a), 1, 0) + contract(x_t[:, 256:], act(k + 3, a), 1, 0)
            out[:, lanes] = total.astype(BF16)
        total = contract(act(k, 0), tokens(g_all, 0), 0, 0) + contract(act(k + 3, 0), tokens(g_all, 1), 0, 0)
        gd[lanes, :] = total.astype(BF16)

    for u in range(3):
        multiply(u)
        scatter(u)
    for u in range(3):
        reduce(u)
        multiply(u + 3)
        scatter(u + 3)
    x_t[...] = x_all[...].reshape(512, 512).T
    forward(0)
    reduce(3)
    forward(1)
    input_grad(0)
    reduce(4)
    forward(2)
    input_grad(1)
    reduce(5)
    input_grad(2)
    forward(3)
    input_grad(3)
    weight_grads(0)
    forward(4)
    input_grad(4)
    weight_grads(1)
    forward(5)
    input_grad(5)
    weight_grads(2)
    outs = [
        pltpu.make_async_copy(src, dst, out_sem.at[i])
        for i, (src, dst) in enumerate([(gg, gg_out), (gu, gu_out), (gd, gd_out), (gi, gi_out)])
    ]
    for out in outs[:3]:
        out.start()
    total = gi_acc[0, :32]
    for i in range(1, 16):
        gi_copies[i].wait_recv()
        total = total + gi_got[i].astype(F32)
    gi[...] = total.astype(BF16)
    outs[3].start()
    for group in (gathers, pairs, scatters, spreads, forwards, gi_copies):
        for copy in group.values():
            copy.wait_send()
    for out in outs:
        out.wait()


def on_device(inputs, out_grad, gate_weight, up_weight, down_weight):
    rows, depth = inputs.shape
    ff = gate_weight.shape[1]
    units = len(UNITS)
    dma = pltpu.SemaphoreType.DMA
    vmem = pltpu.VMEM
    flops = 9 * 2 * 512 * depth * ff
    moved = 2 * 6 * depth * ff
    return pl.pallas_call(
        kernel,
        out_shape=(
            jax.ShapeDtypeStruct(inputs.shape, BF16),
            jax.ShapeDtypeStruct(gate_weight.shape, BF16),
            jax.ShapeDtypeStruct(up_weight.shape, BF16),
            jax.ShapeDtypeStruct(down_weight.shape, BF16),
        ),
        in_specs=[pl.BlockSpec(memory_space=pl.ANY)] * 5,
        out_specs=[pl.BlockSpec(memory_space=pl.ANY)] * 4,
        scratch_shapes=[
            vmem(gate_weight.shape, BF16),
            vmem(up_weight.shape, BF16),
            vmem(down_weight.shape, BF16),
            vmem((16, rows, depth), BF16),
            vmem((16, rows, depth), BF16),
            vmem((depth, 512), BF16),
            vmem((units, 3, 2, 8, 16, CHUNK), F32),
            vmem((units, 3, 8, 16, CHUNK), F32),
            vmem((units, 3, 8, 16, CHUNK), BF16),
            vmem((units, 7, 3, 16, CHUNK), BF16),
            vmem((units, 3, 2, 8, 16, CHUNK), BF16),
            vmem((2, 256, depth), F32),
            vmem((2, 8, rows, depth), BF16),
            vmem((16, rows, depth), BF16),
            vmem(gate_weight.shape, BF16),
            vmem(up_weight.shape, BF16),
            vmem(down_weight.shape, BF16),
            vmem(inputs.shape, BF16),
            dma((5,)),
            dma((16,)),
            dma((16,)),
            dma((16,)),
            dma((16,)),
            dma((units,)),
            dma((units,)),
            dma((units, 7)),
            dma((units, 7)),
            dma((units, 7)),
            dma((units, 7)),
            dma((units,)),
            dma((units,)),
            dma((16,)),
            dma((16,)),
            dma((4,)),
        ],
        compiler_params=pltpu.CompilerParams(
            collective_id=0, has_side_effects=True, vmem_limit_bytes=62 << 20
        ),
        cost_estimate=pl.CostEstimate(flops=flops, bytes_accessed=moved, transcendentals=0),
    )(inputs, out_grad, gate_weight, up_weight, down_weight)


def solution(mesh):
    placed = (P("col", "row"), P("col", "row"), P("row", "col"), P("row", "col"), P("col", "row"))
    return jax.shard_map(
        on_device,
        mesh=mesh,
        in_specs=placed,
        out_specs=(P("col", "row"), P("row", "col"), P("row", "col"), P("col", "row")),
        check_vma=False,
    )
```

time: 438 us -> 131 us (0.30)
  waiting for transfers between devices: 316 us -> 0 us
  Pallas kernels: 0 us -> 114 us
  blocking collectives: 71.7 us -> 0 us
  matrix products: 20.9 us -> 0 us
  local copies, waits for them, and re-layouts: 1.92 us -> 16.5 us
  between operations: 14.1 us -> 0.66 us
  other arithmetic: 11.3 us -> 0 us
    psum x1 -> x0, waiting for transfers between devices: 259 us -> none  [on_device(): summed = lax.psum(stacked, 'row')]
    pallas_call x0 -> x1, Pallas kernels: none -> 114 us  [on_device(): pl.pallas_call(kernel, out_shape=(jax.ShapeDtypeStruct(inputs.shape, BF16...]
    all_gather x2 -> x0, blocking collectives: 71.7 us -> none  [the longest x1 38.8 us: on_device(): lax.all_gather(inputs, 'col', axis=0, tiled=True)]
    reduce_scatter x1 -> x0, waiting for transfers between devices: 57.1 us -> none  [on_device(): lax.psum_scatter(contract_last(dgate, gate_weight) + contract_last(dup, u...]
    dot_general x8 -> x0, matrix products: 20.9 us -> none  [the longest x3 12.2 us: contract_first(): lax.dot_general(left, right, (((0,), (0,)), ((), ())), preferred_element_...]
    unnamed x12 -> x10, local copies, waits for them, and re-layouts: 1.92 us -> 10.1 us
    convert_element_type x2 -> x0, other arithmetic: 6.63 us -> none  [the longest x1 5.18 us: pointwise(): dup = (back * act).astype(jnp.bfloat16)]
    pallas_call x0 -> x2, local copies, waits for them, and re-layouts: none -> 6.37 us  [on_device(): pl.pallas_call(kernel, out_shape=(jax.ShapeDtypeStruct(inputs.shape, BF16...]
  transfers between devices with their start and end apart: 2 -> 0, of which waited for: 2 -> 0; matrix products, arithmetic and copies ran while one was open for 3% -> 0% of each run, Pallas kernels for 0% -> 0%
where the time goes in v1:
time: 131 us
  Pallas kernels  114 us (87%)
  local copies, waits for them, and re-layouts  16.5 us (13%)
    pallas_call x1, Pallas kernels, on_device(): pl.pallas_call(kernel, out_shape=(jax.ShapeDtypeStruct(inputs.shape, BF16...  114 us
    unnamed x10, local copies, waits for them, and re-layouts  10.1 us
    pallas_call x2, local copies, waits for them, and re-layouts, on_device(): pl.pallas_call(kernel, out_shape=(jax.ShapeDtypeStruct(inputs.shape, BF16...  6.37 us

profile of v1, /device:TPU:2, one launch (start us, length us, event | category | flops | bytes accessed | tf_op | source)
XLA Modules:
  0.0 130.8 jit_solution(15607337945623655732)
XLA Ops:
  0.6 0.0 copy-start.1
  0.6 4.1 %copy.9.wg_in = bf16[512,1848]{1,0:T(8,128)(2,1)} copy(bf16[512,1848]{0,1:T(8,128)(2,1)} %param.7) | data formatting | bytes 3784704 | tf_op args[2]
  4.7 0.0 copy-done.1
  4.7 2.5 %copy.10.wu_in = bf16[512,1848]{1,0:T(8,128)(2,1)} copy(bf16[512,1848]{0,1:T(8,128)(2,1)S(1)} %copy-done.1) | data formatting | bytes 3784704 | tf_op args[3]
  7.2 113.6 %shard_map.84 = (bf16[32,512]{1,0:T(8,128)(2,1)}, bf16[512,1848]{1,0:T(8,128)(2,1)}, bf16[512,1848]{1,0:T(8,128)(2,1)}, bf16[1848,512]{1,0:T(8,128)(2,1)}) custom-call(bf16[32,512]{1,0:T(8,128)(2,1)} %x_in.1, bf16[32,512]{1,0:T(8,128)(2,1)} %g_in.1, bf16[512,1848]{1,0:T(8,128)(2,1)} %copy.9.wg_in, bf16[512,1848]{1,0:T(8,128)(2,1)} %copy.10.wu_in, ...), custom_call_target="tpu_custom_call" | custom-call | flops 8719958016 | bytes 11354112 | tf_op jit(solution)/shard_map/pallas_call | solution.py:252
  120.9 0.0 copy-start
  120.9 4.1 %copy.11 = bf16[512,1848]{0,1:T(8,128)(2,1)} copy(bf16[512,1848]{1,0:T(8,128)(2,1)} %get-tuple-element.5) | data formatting | bytes 3784704 | tf_op jit(solution)/shard_map/pallas_call | solution.py:252
  125.0 0.0 copy-done
  125.0 0.0 copy-start.2
  125.0 2.3 %copy.12 = bf16[512,1848]{0,1:T(8,128)(2,1)} copy(bf16[512,1848]{1,0:T(8,128)(2,1)S(1)} %copy-done) | data formatting | bytes 3784704 | tf_op jit(solution)/shard_map/pallas_call | solution.py:252
  127.3 0.0 copy-done.2
  127.3 0.6 copy.15
  127.9 2.9 %copy.16 = bf16[1848,512]{1,0:T(8,128)(2,1)} copy(bf16[1848,512]{1,0:T(8,128)(2,1)} %get-tuple-element.15) | data formatting | bytes 3784704
Async XLA Ops:
  0.6 4.1 %copy-start.1 = (bf16[512,1848]{0,1:T(8,128)(2,1)S(1)}, bf16[512,1848]{0,1:T(8,128)(2,1)}, u32[]{:S(2)}) copy-start(bf16[512,1848]{0,1:T(8,128)(2,1)} %param.8) | copy-start | bytes 5677060
  120.9 4.1 %copy-start = (bf16[512,1848]{1,0:T(8,128)(2,1)S(1)}, bf16[512,1848]{1,0:T(8,128)(2,1)}, u32[]{:S(2)}) copy-start(bf16[512,1848]{1,0:T(8,128)(2,1)} %get-tuple-element.6) | copy-start | bytes 5677060
  125.0 2.3 %copy-start.2 = (bf16[32,512]{1,0:T(8,128)(2,1)S(1)}, bf16[32,512]{1,0:T(8,128)(2,1)}, u32[]{:S(2)}) copy-start(bf16[32,512]{1,0:T(8,128)(2,1)} %get-tuple-element.12) | copy-start | bytes 98308

commit v2 on v0

v2 whole, which is shorter than its diff:
```python
import functools

import jax
import jax.numpy as jnp
from jax import lax
from jax.experimental import pallas as pl
from jax.experimental.pallas import tpu as pltpu
from jax.sharding import PartitionSpec as P

MESH = pl.DeviceIdType.MESH
F32, BF16 = jnp.float32, jnp.bfloat16

NEAR = [(0, 0), (0, 1), (1, 0), (1, 1), (-1, 0), (-1, 1), (2, 0), (-2, 0)]
NEAR += [(2, 1), (-2, 1), (3, 0), (3, 1), (-3, 0), (-3, 1), (4, 0), (4, 1)]
CHUNK = 640
UNITS = [(g, k) for g in range(2) for k in range(3)]
SUM_Y_FIRST = (False, True, False, False, False, True)
SPREAD_X_FIRST = (True, True, False, True, False, True)


def contract(left, right, left_dim, right_dim):
    return lax.dot_general(
        left,
        right,
        (((left_dim,), (right_dim,)), ((), ())),
        preferred_element_type=F32,
    )


def pointwise(gate, up, back):
    sig = jax.nn.sigmoid(gate)
    act = gate * sig
    hidden = act * up
    dgate = back * up * sig * (1.0 + gate * (1.0 - sig))
    dup = back * act
    return hidden.astype(BF16), dgate.astype(BF16), dup.astype(BF16)


def kernel(
    x_in, g_in, wg_in, wu_in, wd_in,
    gi_out, gg_out, gu_out, gd_out,
    wg, wu, wd, x_all, g_all, part, pair, terms, got, mid, cross, got_cross,
    acts, gi_acc, gi_send, gi_got, gg, gu, gd, gi,
    w_sem, near_send, near_recv, pair_send, pair_recv, sum_send, cross_send, sum_recv,
    act_send, act_recv, half_send, half_recv, gi_ssem, gi_rsem, out_sem,
):
    row, col = lax.axis_index("row"), lax.axis_index("col")
    y, h, c = row // 4, (row // 2) % 2, row % 2
    xl, z = col // 8, col % 8
    ff = wg.shape[0]

    def along(dy):
        return (y + dy) % 4

    def owner_at(dy, dh):
        return {"row": (along(dy) * 2 + (h + dh) % 2) * 2 + c, "col": col}

    def near_at(dz, dx):
        return {"row": row, "col": ((xl + dx) % 2) * 8 + (z + dz + 8) % 8}

    partner = {"row": row + 1 - 2 * c, "col": col}
    across = owner_at(0, 1)

    def remote(src, dst, send, recv, to):
        return pltpu.make_async_remote_copy(
            src_ref=src, dst_ref=dst, send_sem=send, recv_sem=recv, device_id=to, device_id_type=MESH
        )

    def settle(ref, sem):
        remote(ref, ref, sem, sem, partner).wait_recv()

    def width(k):
        return min(CHUNK, ff - k * CHUNK)

    loads = [
        pltpu.make_async_copy(src, dst, w_sem.at[i])
        for i, (src, dst) in enumerate(
            [(x_in, x_all.at[0]), (g_in, g_all.at[0]), (wg_in, wg), (wu_in, wu), (wd_in, wd)]
        )
    ]
    for load in loads:
        load.start()

    with jax.named_scope("greet"):
      barrier = pltpu.get_barrier_semaphore()
    peers = [partner, across] + [owner_at(dy, 0) for dy in (1, 2, 3)]
    peers += [near_at(0, 1), near_at(1, 0), near_at(-1, 0)]
    for peer in peers:
        pl.semaphore_signal(barrier, inc=1, device_id=peer, device_id_type=MESH)
    pl.semaphore_wait(barrier, len(peers))

    def hand(n, slot, to, at):
        ref = (x_all, g_all)[n]
        src = (x_in, g_in)[n] if slot == 0 else ref.at[slot]
        remote(src, ref.at[at], near_send.at[n], near_recv.at[n, at], to).start()

    seen = set()

    def arrived(n, slot):
        ref = (x_all, g_all)[n]
        if (n, slot) not in seen:
            seen.add((n, slot))
            if slot:
                remote(ref.at[slot], ref.at[slot], near_send.at[n], near_recv.at[n, slot], partner).wait_recv()
            else:
                loads[n].wait()

    def slot_of(dz, dx):
        return NEAR.index((dz, dx))

    def gather(step, n):
        if step == 0:
            hand(n, 0, near_at(0, 1), slot_of(0, 1))
        dx = step % 2
        far = step // 2
        for way in (1, -1):
            if far == 3 and (way == 1) == bool(dx):
                continue
            slot = slot_of(-way * far, dx)
            if slot:
                arrived(n, slot)
        for way in (1, -1):
            if far == 3 and (way == 1) == bool(dx):
                continue
            to = -way * (far + 1) if far < 3 else 4
            hand(n, slot_of(-way * far, dx), near_at(way, 0), slot_of(to, dx))

    def landed(n, group):
        for slot in range(group * 8, group * 8 + 8):
            arrived(n, slot)

    def tokens(ref, group):
        return ref[group * 8 : group * 8 + 8].reshape(256, 512)

    def multiply(u, a, ref, weight):
        g, k = UNITS[u]
        w = width(k)
        if w < CHUNK:
            part[u, a, :, :, :, :, CHUNK - 128 :] = jnp.zeros((2, 2, 4, 16, 128), F32)
        product = contract(tokens(ref, g), weight[k * CHUNK : k * CHUNK + w, :], 1, 1)
        part[u, a, :, :, :, :, :w] = product.reshape(2, 2, 4, 16, w)
        remote(part.at[u, a, 1 - c], pair.at[u, a], pair_send.at[0], pair_recv.at[u], partner).start()

    def gate_up(u):
        g, k = UNITS[u]
        if k == 0:
            landed(0, g)
        if u == 0:
            loads[2].wait()
        multiply(u, 0, x_all, wg)
        if u == 0:
            loads[3].wait()
        multiply(u, 1, x_all, wu)

    def back(u):
        g, k = UNITS[u]
        if k == 0:
            landed(1, g)
        if u == 0:
            loads[4].wait()
        multiply(u, 2, g_all, wd)

    def sum_first(u):
        settle(pair.at[u], pair_recv.at[u])
        for a in range(3):
            if SUM_Y_FIRST[u]:
                terms[u, :, :, a] = (part[u, a, c] + pair[u, a]).astype(BF16)
            else:
                terms[u, 1 - h, :, a] = (part[u, a, c, 1 - h] + pair[u, a, 1 - h]).astype(BF16)
        if SUM_Y_FIRST[u]:
            for dy in (2, 1, 3):
                remote(
                    terms.at[u, :, along(dy)], got.at[u, 2 * dy - 2 : 2 * dy],
                    sum_send.at[u], sum_recv.at[u, 0], owner_at(dy, 0),
                ).start()
        else:
            remote(terms.at[u, 1 - h], got.at[u, :4], sum_send.at[u], sum_recv.at[u, 0], across).start()

    def sum_second(u):
        if SUM_Y_FIRST[u]:
            settle(got.at[u, :6], sum_recv.at[u, 0])
            n = sum(SUM_Y_FIRST[:u])
            for a in range(3):
                total = part[u, a, c, 1 - h, y] + pair[u, a, 1 - h, y]
                for i in range(3):
                    total = total + got[u, 2 * i + 1 - h, a].astype(F32)
                cross[n, a] = total
            remote(cross.at[n], got_cross.at[n], cross_send.at[0], sum_recv.at[u, 1], across).start()
        else:
            settle(got.at[u, :4], sum_recv.at[u, 0])
            for a in range(3):
                total = part[u, a, c, h] + pair[u, a, h] + got[u, :4, a].astype(F32)
                mid[u, :, a] = total.astype(BF16)
            for dy in (2, 1, 3):
                remote(
                    mid.at[u, along(dy)], got.at[u, 3 + dy], sum_send.at[u], sum_recv.at[u, 1], owner_at(dy, 0)
                ).start()

    def block(u, dy, dh, arrays=slice(0, 3)):
        return acts.at[u, arrays, c, (h + dh) % 2, along(dy)]

    def spread(u, sem, ref, to):
        remote(ref, ref, act_send.at[u], act_recv.at[u, sem], to).start()

    def reduce(u):
        totals = []
        n = sum(SUM_Y_FIRST[:u])
        if SUM_Y_FIRST[u]:
            settle(got_cross.at[n], sum_recv.at[u, 1])
        else:
            settle(got.at[u, 4:7], sum_recv.at[u, 1])
        for a in range(3):
            total = part[u, a, c, h, y] + pair[u, a, h, y]
            if SUM_Y_FIRST[u]:
                for i in range(3):
                    total = total + got[u, 2 * i + h, a].astype(F32)
                total = total + got_cross[n, a]
            else:
                total = total + got[u, y, a].astype(F32)
                for i in range(3):
                    total = total + got[u, 4 + i, a].astype(F32)
            totals.append(total)
        for a, value in enumerate(pointwise(*totals)):
            acts[u, a, c, h, y] = value
        own = block(u, 0, 0)
        if SPREAD_X_FIRST[u]:
            spread(u, 0, own, across)
            spread(u, 1, own, owner_at(1, 0))
            spread(u, 3, own, owner_at(3, 0))
        else:
            spread(u, 0, own, owner_at(1, 0))
            spread(u, 1, own, owner_at(3, 0))
            spread(u, 3, own, across)

    def spread_a(u):
        settle(block(u, 0, 0), act_recv.at[u, 0])
        if SPREAD_X_FIRST[u]:
            spread(u, 3, block(u, 0, 1), owner_at(1, 0))
            spread(u, 2, block(u, 0, 1), owner_at(3, 0))
        else:
            spread(u, 2, block(u, 3, 0, slice(0, 2)), owner_at(1, 0))
            spread(u, 3, block(u, 3, 0), across)

    def spread_b(u):
        settle(block(u, 0, 0), act_recv.at[u, 1])
        if SPREAD_X_FIRST[u]:
            spread(u, 3, block(u, 3, 0), owner_at(1, 0))
        else:
            spread(u, 2, block(u, 1, 0, slice(2, 3)), owner_at(3, 0))
            spread(u, 3, block(u, 1, 0), across)

    def spread_c(u):
        settle(block(u, 0, 0), act_recv.at[u, 2])
        if SPREAD_X_FIRST[u]:
            spread(u, 3, block(u, 1, 1), owner_at(3, 0))
        else:
            spread(u, 3, block(u, 2, 0), across)

    def spread_last(u):
        settle(got.at[u, :4], act_recv.at[u, 3])
        half = acts.at[u, :, c]
        remote(half, half, half_send.at[0], half_recv.at[u], partner).start()

    def act(u, a):
        return acts[u, a].reshape(256, CHUNK)[:, : width(UNITS[u][1])]

    def input_grad(u):
        g, k = UNITS[u]
        rows = slice(k * CHUNK, k * CHUNK + width(k))
        settle(acts.at[u, :, 1 - c], half_recv.at[u])
        term = contract(act(u, 1), wg[rows, :], 1, 0) + contract(act(u, 2), wu[rows, :], 1, 0)
        if k > 0:
            term = term + gi_acc[g]
        gi_acc[g] = term
        if k == 2:
            gi_send[g] = term.astype(BF16).reshape(8, 32, 512)
            for b in reversed(range(8)):
                i = g * 8 + b
                if i:
                    remote(gi_send.at[g, b], gi_got.at[i], gi_ssem.at[0], gi_rsem.at[0], near_at(*NEAR[i])).start()

    def weight_grads(k):
        rows = slice(k * CHUNK, k * CHUNK + width(k))
        for a, ref, out in ((1, x_all, gg), (2, x_all, gu), (0, g_all, gd)):
            total = contract(act(k, a), tokens(ref, 0), 0, 0) + contract(act(k + 3, a), tokens(ref, 1), 0, 0)
            out[rows, :] = total.astype(BF16)

    plan = [
        (gather, 0, 0), (gather, 0, 1), (gather, 1, 0), (gather, 1, 1),
        (gather, 2, 0), (gather, 2, 1), (gather, 3, 0), (gather, 3, 1),
        (gate_up, 0), (gate_up, 1), (gather, 4, 0), (gather, 4, 1),
        (back, 0), (back, 1), (gather, 5, 0), (gather, 5, 1),
        (gate_up, 2), (back, 2), (gather, 6, 0), (gather, 6, 1),
        (sum_first, 0), (gather, 7, 0), (gather, 7, 1), (sum_first, 1),
        (sum_first, 2), (gate_up, 3), (gate_up, 4), (back, 3),
        (back, 4), (gate_up, 5), (back, 5), (sum_first, 3),
        (sum_second, 0), (sum_second, 1), (sum_first, 4), (sum_first, 5),
        (reduce, 0), (sum_second, 2), (sum_second, 3), (reduce, 1),
        (reduce, 2), (reduce, 3), (sum_second, 4), (sum_second, 5),
        (spread_a, 0), (spread_b, 0), (spread_a, 1), (spread_b, 1),
        (spread_a, 2), (spread_b, 2), (reduce, 4), (spread_a, 3),
        (spread_b, 3), (spread_c, 0), (reduce, 5), (spread_c, 1),
        (spread_c, 2), (spread_a, 4), (spread_b, 4), (spread_c, 3),
        (spread_a, 5), (spread_last, 0), (spread_b, 5), (input_grad, 0),
        (spread_last, 1), (spread_last, 2), (spread_c, 4), (spread_last, 3),
        (input_grad, 1), (spread_c, 5), (input_grad, 2), (input_grad, 3),
        (spread_last, 4), (weight_grads, 0), (spread_last, 5), (input_grad, 4),
        (weight_grads, 1), (input_grad, 5), (weight_grads, 2),
    ]
    for stage, *at in plan:
        stage(*at)
    outs = [
        pltpu.make_async_copy(src, dst, out_sem.at[i])
        for i, (src, dst) in enumerate([(gg, gg_out), (gu, gu_out), (gd, gd_out), (gi, gi_out)])
    ]
    for out in outs[:3]:
        out.start()
    settle(gi_got.at[1:16], gi_rsem.at[0])
    total = gi_acc[0, :32]
    for i in range(1, 16):
        total = total + gi_got[i].astype(F32)
    gi[...] = total.astype(BF16)
    outs[3].start()
    settle(x_all.at[1:16], near_send.at[0])
    settle(g_all.at[1:16], near_send.at[1])
    settle(pair, pair_send.at[0])
    for u in range(len(UNITS)):
        settle(got.at[u, : 6 if SUM_Y_FIRST[u] else 7], sum_send.at[u])
        settle(got.at[u], act_send.at[u])
    settle(cross, cross_send.at[0])
    settle(terms, half_send.at[0])
    settle(gi_got.at[1:16], gi_ssem.at[0])
    for out in outs:
        out.wait()


def place(*refs):
    count = (len(refs) - 2) // 3
    sources, results, held = refs[:count], refs[count : 2 * count], refs[2 * count : 3 * count]
    ins = [pltpu.make_async_copy(a, b, refs[-2].at[i]) for i, (a, b) in enumerate(zip(sources, held))]
    outs = [pltpu.make_async_copy(a, b, refs[-1].at[i]) for i, (a, b) in enumerate(zip(held, results))]
    for copy in ins:
        copy.start()
    for taken, given in zip(ins, outs):
        taken.wait()
        given.start()
    for copy in outs:
        copy.wait()


def on_device(inputs, out_grad, gate_weight, up_weight, down_weight):
    rows, depth = inputs.shape
    gate_weight, up_weight = gate_weight.T, up_weight.T
    ff = gate_weight.shape[0]
    units = len(UNITS)
    dma = pltpu.SemaphoreType.DMA
    vmem = pltpu.VMEM
    weight = jax.ShapeDtypeStruct((ff, depth), BF16)
    results = (jax.ShapeDtypeStruct(inputs.shape, BF16), weight, weight, weight)
    anywhere = pl.BlockSpec(memory_space=pl.ANY)
    made = pl.pallas_call(
        kernel,
        out_shape=results,
        in_specs=[anywhere] * 5,
        out_specs=[anywhere] * 4,
        scratch_shapes=[
            vmem((ff, depth), BF16),
            vmem((ff, depth), BF16),
            vmem((ff, depth), BF16),
            vmem((16, rows, depth), BF16),
            vmem((16, rows, depth), BF16),
            vmem((units, 3, 2, 2, 4, 16, CHUNK), F32),
            vmem((units, 3, 2, 4, 16, CHUNK), F32),
            vmem((units, 2, 4, 3, 16, CHUNK), BF16),
            vmem((units, 7, 3, 16, CHUNK), BF16),
            vmem((units, 4, 3, 16, CHUNK), BF16),
            vmem((sum(SUM_Y_FIRST), 3, 16, CHUNK), F32),
            vmem((sum(SUM_Y_FIRST), 3, 16, CHUNK), F32),
            vmem((units, 3, 2, 2, 4, 16, CHUNK), BF16),
            vmem((2, 256, depth), F32),
            vmem((2, 8, rows, depth), BF16),
            vmem((16, rows, depth), BF16),
            vmem((ff, depth), BF16),
            vmem((ff, depth), BF16),
            vmem((ff, depth), BF16),
            vmem(inputs.shape, BF16),
            dma((5,)),
            dma((2,)),
            dma((2, 16)),
            dma((1,)),
            dma((units,)),
            dma((units,)),
            dma((1,)),
            dma((units, 2)),
            dma((units,)),
            dma((units, 4)),
            dma((1,)),
            dma((units,)),
            dma((1,)),
            dma((1,)),
            dma((4,)),
        ],
        compiler_params=pltpu.CompilerParams(
            collective_id=0, has_side_effects=True, vmem_limit_bytes=62 << 20
        ),
        cost_estimate=pl.CostEstimate(
            flops=18 * 512 * depth * ff, bytes_accessed=12 * depth * ff, transcendentals=0
        ),
    )(inputs, out_grad, gate_weight, up_weight, down_weight)
    grad_input, grad_gate, grad_up, grad_down = pl.pallas_call(
        place,
        out_shape=results,
        in_specs=[anywhere] * 4,
        out_specs=[anywhere] * 4,
        scratch_shapes=[vmem(a.shape, a.dtype) for a in results] + [dma((4,)), dma((4,))],
        compiler_params=pltpu.CompilerParams(vmem_limit_bytes=60 << 20),
    )(*made)
    return grad_input, grad_gate.T, grad_up.T, grad_down


def solution(mesh):
    placed = (P("col", "row"), P("col", "row"), P("row", "col"), P("row", "col"), P("col", "row"))
    return jax.shard_map(
        on_device,
        mesh=mesh,
        in_specs=placed,
        out_specs=(P("col", "row"), P("row", "col"), P("row", "col"), P("col", "row")),
        check_vma=False,
    )
```

time: 438 us -> 93.3 us (0.21)
  waiting for transfers between devices: 316 us -> 0 us
  Pallas kernels: 0 us -> 92 us
  blocking collectives: 71.7 us -> 0 us
  matrix products: 20.9 us -> 0 us
  between operations: 14.1 us -> 0.64 us
  other arithmetic: 11.3 us -> 0 us
    psum x1 -> x0, waiting for transfers between devices: 259 us -> none  [on_device(): summed = lax.psum(stacked, 'row')]
    pallas_call x0 -> x2, Pallas kernels: none -> 92 us  [the longest x1 87.5 us: on_device(): pl.pallas_call(kernel, out_shape=results, in_specs=[anywhere] * 5, out_sp...]
    all_gather x2 -> x0, blocking collectives: 71.7 us -> none  [the longest x1 38.8 us: on_device(): lax.all_gather(inputs, 'col', axis=0, tiled=True)]
    reduce_scatter x1 -> x0, waiting for transfers between devices: 57.1 us -> none  [on_device(): lax.psum_scatter(contract_last(dgate, gate_weight) + contract_last(dup, u...]
    dot_general x8 -> x0, matrix products: 20.9 us -> none  [the longest x3 12.2 us: contract_first(): lax.dot_general(left, right, (((0,), (0,)), ((), ())), preferred_element_...]
    convert_element_type x2 -> x0, other arithmetic: 6.63 us -> none  [the longest x1 5.18 us: pointwise(): dup = (back * act).astype(jnp.bfloat16)]
    another operation x1 -> x0, other arithmetic: 4.65 us -> none  [on_device(): stacked = jnp.stack([gate_part, up_part, back_part])]
  transfers between devices with their start and end apart: 2 -> 0, of which waited for: 2 -> 0; matrix products, arithmetic and copies ran while one was open for 3% -> 0% of each run, Pallas kernels for 0% -> 0%
where the time goes in v2:
time: 93.3 us; the launch traced here: 92.6 us
  Pallas kernels  92 us (99%)
    pallas_call x1, Pallas kernels, on_device(): pl.pallas_call(kernel, out_shape=results, in_specs=[anywhere] * 5, out_sp...  87.5 us
    pallas_call x1, Pallas kernels, on_device(): pl.pallas_call(place, out_shape=results, in_specs=[anywhere] * 4, out_spe...  4.43 us

profile of v2, /device:TPU:2, one launch (start us, length us, event | category | flops | bytes accessed | tf_op | source)
XLA Modules:
  0.0 92.6 jit_solution(1471802749249539800)
XLA Ops:
  0.6 87.5 %shard_map.84 = (bf16[32,512]{1,0:T(8,128)(2,1)}, bf16[1848,512]{1,0:T(8,128)(2,1)}, bf16[1848,512]{1,0:T(8,128)(2,1)}, bf16[1848,512]{1,0:T(8,128)(2,1)}) custom-call(bf16[32,512]{1,0:T(8,128)(2,1)} %x_in.1, bf16[32,512]{1,0:T(8,128)(2,1)} %g_in.1, bf16[1848,512]{1,0:T(8,128)(2,1)} %bitcast.4, bf16[1848,512]{1,0:T(8,128)(2,1)} %bitcast.5, ...), custom_call_target="tpu_custom_call" | custom-call | flops 8719958016 | bytes 11354112 | tf_op jit(solution)/shard_map/pallas_call | solution.py:361
  88.2 4.4 %shard_map.85 = (bf16[32,512]{1,0:T(8,128)(2,1)}, bf16[1848,512]{1,0:T(8,128)(2,1)}, bf16[1848,512]{1,0:T(8,128)(2,1)}, bf16[1848,512]{1,0:T(8,128)(2,1)}) custom-call(bf16[32,512]{1,0:T(8,128)(2,1)} %get-tuple-element.12.refs_0_, bf16[1848,512]{1,0:T(8,128)(2,1)} %get-tuple-element.13.refs_1_, bf16[1848,512]{1,0:T(8,128)(2,1)} %get-tuple-element.14.refs_2_, ...), custom_call_target="tpu_custom_call" | custom-call | tf_op jit(solution)/shard_map/pallas_call | solution.py:410

commit v3 on v2

--- a/solution.py
+++ b/solution.py
@@ -14,8 +14,8 @@
 NEAR += [(2, 1), (-2, 1), (3, 0), (3, 1), (-3, 0), (-3, 1), (4, 0), (4, 1)]
 CHUNK = 640
 UNITS = [(g, k) for g in range(2) for k in range(3)]
-SUM_Y_FIRST = (False, True, False, False, False, True)
-SPREAD_X_FIRST = (True, True, False, True, False, True)
+SUM_Y_FIRST = (True, False, True, False, False, True)
+SPREAD_X_FIRST = (True, True, False, False, True, True)
 
 
 def contract(left, right, left_dim, right_dim):
@@ -84,15 +84,14 @@
     with jax.named_scope("greet"):
       barrier = pltpu.get_barrier_semaphore()
     peers = [partner, across] + [owner_at(dy, 0) for dy in (1, 2, 3)]
-    peers += [near_at(0, 1), near_at(1, 0), near_at(-1, 0)]
+    peers += [near_at(*step) for step in NEAR[1:8]]
     for peer in peers:
         pl.semaphore_signal(barrier, inc=1, device_id=peer, device_id_type=MESH)
     pl.semaphore_wait(barrier, len(peers))
 
     def hand(n, slot, to, at):
         ref = (x_all, g_all)[n]
-        src = (x_in, g_in)[n] if slot == 0 else ref.at[slot]
-        remote(src, ref.at[at], near_send.at[n], near_recv.at[n, at], to).start()
+        remote(ref.at[slot], ref.at[at], near_send.at[n], near_recv.at[n, at], to).start()
 
     seen = set()
 
@@ -108,22 +107,26 @@
     def slot_of(dz, dx):
         return NEAR.index((dz, dx))
 
-    def gather(step, n):
-        if step == 0:
-            hand(n, 0, near_at(0, 1), slot_of(0, 1))
-        dx = step % 2
-        far = step // 2
+    def gather_near(n):
+        arrived(n, 0)
+        for slot in (6, 7, 3, 5, 2, 4, 1):
+            dz, dx = NEAR[slot]
+            hand(n, 0, near_at(-dz, dx), slot)
+
+    def gather(far, dx, n):
         for way in (1, -1):
             if far == 3 and (way == 1) == bool(dx):
                 continue
             slot = slot_of(-way * far, dx)
-            if slot:
-                arrived(n, slot)
-        for way in (1, -1):
-            if far == 3 and (way == 1) == bool(dx):
-                continue
-            to = -way * (far + 1) if far < 3 else 4
-            hand(n, slot_of(-way * far, dx), near_at(way, 0), slot_of(to, dx))
+            arrived(n, slot)
+            hand(n, slot, near_at(way, 0), slot_of(-way * (far + 1) if far < 3 else 4, dx))
+
+    loaded = set()
+
+    def weights_in(n):
+        if n not in loaded:
+            loaded.add(n)
+            loads[n].wait()
 
     def landed(n, group):
         for slot in range(group * 8, group * 8 + 8):
@@ -142,22 +145,15 @@
         remote(part.at[u, a, 1 - c], pair.at[u, a], pair_send.at[0], pair_recv.at[u], partner).start()
 
     def gate_up(u):
-        g, k = UNITS[u]
-        if k == 0:
-            landed(0, g)
-        if u == 0:
-            loads[2].wait()
+        landed(0, UNITS[u][0])
+        weights_in(2)
         multiply(u, 0, x_all, wg)
-        if u == 0:
-            loads[3].wait()
+        weights_in(3)
         multiply(u, 1, x_all, wu)
 
     def back(u):
-        g, k = UNITS[u]
-        if k == 0:
-            landed(1, g)
-        if u == 0:
-            loads[4].wait()
+        landed(1, UNITS[u][0])
+        weights_in(4)
         multiply(u, 2, g_all, wd)
 
     def sum_first(u):
@@ -264,15 +260,18 @@
     def act(u, a):
         return acts[u, a].reshape(256, CHUNK)[:, : width(UNITS[u][1])]
 
+    summed = [0, 0]
+
     def input_grad(u):
         g, k = UNITS[u]
         rows = slice(k * CHUNK, k * CHUNK + width(k))
         settle(acts.at[u, :, 1 - c], half_recv.at[u])
         term = contract(act(u, 1), wg[rows, :], 1, 0) + contract(act(u, 2), wu[rows, :], 1, 0)
-        if k > 0:
+        if summed[g] > 0:
             term = term + gi_acc[g]
         gi_acc[g] = term
-        if k == 2:
+        summed[g] += 1
+        if summed[g] == 3:
             gi_send[g] = term.astype(BF16).reshape(8, 32, 512)
             for b in reversed(range(8)):
                 i = g * 8 + b
@@ -286,26 +285,26 @@
             out[rows, :] = total.astype(BF16)
 
     plan = [
-        (gather, 0, 0), (gather, 0, 1), (gather, 1, 0), (gather, 1, 1),
-        (gather, 2, 0), (gather, 2, 1), (gather, 3, 0), (gather, 3, 1),
-        (gate_up, 0), (gate_up, 1), (gather, 4, 0), (gather, 4, 1),
-        (back, 0), (back, 1), (gather, 5, 0), (gather, 5, 1),
-        (gate_up, 2), (back, 2), (gather, 6, 0), (gather, 6, 1),
-        (sum_first, 0), (gather, 7, 0), (gather, 7, 1), (sum_first, 1),
-        (sum_first, 2), (gate_up, 3), (gate_up, 4), (back, 3),
-        (back, 4), (gate_up, 5), (back, 5), (sum_first, 3),
-        (sum_second, 0), (sum_second, 1), (sum_first, 4), (sum_first, 5),
-        (reduce, 0), (sum_second, 2), (sum_second, 3), (reduce, 1),
-        (reduce, 2), (reduce, 3), (sum_second, 4), (sum_second, 5),
-        (spread_a, 0), (spread_b, 0), (spread_a, 1), (spread_b, 1),
-        (spread_a, 2), (spread_b, 2), (reduce, 4), (spread_a, 3),
-        (spread_b, 3), (spread_c, 0), (reduce, 5), (spread_c, 1),
-        (spread_c, 2), (spread_a, 4), (spread_b, 4), (spread_c, 3),
-        (spread_a, 5), (spread_last, 0), (spread_b, 5), (input_grad, 0),
-        (spread_last, 1), (spread_last, 2), (spread_c, 4), (spread_last, 3),
-        (input_grad, 1), (spread_c, 5), (input_grad, 2), (input_grad, 3),
-        (spread_last, 4), (weight_grads, 0), (spread_last, 5), (input_grad, 4),
-        (weight_grads, 1), (input_grad, 5), (weight_grads, 2),
+        (gather_near, 0), (gather_near, 1),
+        (gather, 1, 1, 0), (gate_up, 0), (gather, 2, 0, 0), (gate_up, 1),
+        (gather, 1, 1, 1), (back, 0), (gather, 2, 0, 1), (back, 1),
+        (gather, 2, 1, 0), (gather, 3, 0, 0), (gate_up, 2), (back, 2),
+        (gather, 2, 1, 1), (gather, 3, 0, 1), (sum_first, 0), (sum_first, 1),
+        (gather, 3, 1, 0), (gather, 3, 1, 1), (sum_first, 2), (gate_up, 3),
+        (gate_up, 5), (gate_up, 4), (sum_second, 0), (back, 3),
+        (back, 5), (sum_second, 1), (back, 4), (sum_first, 3),
+        (sum_first, 5), (sum_first, 4), (sum_second, 2), (reduce, 0),
+        (reduce, 1), (sum_second, 3), (sum_second, 5), (sum_second, 4),
+        (reduce, 2), (reduce, 3), (spread_a, 0), (spread_b, 0),
+        (spread_a, 1), (spread_b, 1), (reduce, 4), (spread_a, 2),
+        (spread_b, 2), (reduce, 5), (spread_a, 3), (spread_b, 3),
+        (spread_c, 0), (spread_c, 1), (spread_a, 4), (spread_b, 4),
+        (spread_c, 2), (spread_c, 3), (spread_a, 5), (spread_b, 5),
+        (spread_last, 0), (spread_last, 1), (input_grad, 0), (spread_c, 4),
+        (input_grad, 1), (spread_last, 2), (spread_c, 5), (spread_last, 3),
+        (input_grad, 2), (spread_last, 4), (input_grad, 3), (spread_last, 5),
+        (weight_grads, 0), (input_grad, 4), (input_grad, 5), (weight_grads, 2),
+        (weight_grads, 1),
     ]
     for stage, *at in plan:
         stage(*at)
@@ -335,17 +334,8 @@
 
 
 def place(*refs):
-    count = (len(refs) - 2) // 3
-    sources, results, held = refs[:count], refs[count : 2 * count], refs[2 * count : 3 * count]
-    ins = [pltpu.make_async_copy(a, b, refs[-2].at[i]) for i, (a, b) in enumerate(zip(sources, held))]
-    outs = [pltpu.make_async_copy(a, b, refs[-1].at[i]) for i, (a, b) in enumerate(zip(held, results))]
-    for copy in ins:
-        copy.start()
-    for taken, given in zip(ins, outs):
-        taken.wait()
-        given.start()
-    for copy in outs:
-        copy.wait()
+    for source, result in zip(refs[:4], refs[4:]):
+        result[...] = source[...]
 
 
 def on_device(inputs, out_grad, gate_weight, up_weight, down_weight):
@@ -401,19 +391,21 @@
             dma((4,)),
         ],
         compiler_params=pltpu.CompilerParams(
-            collective_id=0, has_side_effects=True, vmem_limit_bytes=62 << 20
+            collective_id=0, has_side_effects=True, vmem_limit_bytes=48 << 20
         ),
         cost_estimate=pl.CostEstimate(
             flops=18 * 512 * depth * ff, bytes_accessed=12 * depth * ff, transcendentals=0
         ),
-    )(inputs, out_grad, gate_weight, up_weight, down_weight)
+    )(*(pltpu.with_memory_space_constraint(a, pltpu.HBM) for a in (inputs, out_grad)), gate_weight, up_weight, down_weight)
+    part = pl.BlockSpec((616, depth), lambda i: (i, 0))
+    specs = [pl.BlockSpec(inputs.shape, lambda i: (0, 0))] + [part] * 3
     grad_input, grad_gate, grad_up, grad_down = pl.pallas_call(
         place,
+        grid=(pl.cdiv(ff, 616),),
         out_shape=results,
-        in_specs=[anywhere] * 4,
-        out_specs=[anywhere] * 4,
-        scratch_shapes=[vmem(a.shape, a.dtype) for a in results] + [dma((4,)), dma((4,))],
-        compiler_params=pltpu.CompilerParams(vmem_limit_bytes=60 << 20),
+        in_specs=specs,
+        out_specs=specs,
+        compiler_params=pltpu.CompilerParams(vmem_limit_bytes=10 << 20),
     )(*made)
     return grad_input, grad_gate.T, grad_up.T, grad_down
 

time: 93.3 us -> 87.5 us (0.938)
  Pallas kernels: 92 us -> 85.8 us
    pallas_call x1, Pallas kernels: 87.5 us -> 83 us  [on_device(): pl.pallas_call(kernel, out_shape=results, in_specs=[anywhere] * 5, out_sp...]
    pallas_call x1, Pallas kernels: 4.43 us -> 2.76 us  [on_device(): pl.pallas_call(place, grid=(pl.cdiv(ff, 616),), out_shape=results, in_spe...]
where the time goes in v3:
time: 87.5 us; the launch traced here: 86.4 us
  Pallas kernels  85.8 us (98%)
    pallas_call x1, Pallas kernels, on_device(): pl.pallas_call(kernel, out_shape=results, in_specs=[anywhere] * 5, out_sp...  83 us
    pallas_call x1, Pallas kernels, on_device(): pl.pallas_call(place, grid=(pl.cdiv(ff, 616),), out_shape=results, in_spe...  2.76 us

profile of v3, /device:TPU:2, one launch (start us, length us, event | category | flops | bytes accessed | tf_op | source)
XLA Modules:
  0.0 86.4 jit_solution(4372375664663191543)
XLA Ops:
  0.6 83.0 %shard_map.84 = (bf16[32,512]{1,0:T(8,128)(2,1)S(1)}, bf16[1848,512]{1,0:T(8,128)(2,1)S(1)}, bf16[1848,512]{1,0:T(8,128)(2,1)S(1)}, bf16[1848,512]{1,0:T(8,128)(2,1)S(1)}) custom-call(bf16[32,512]{1,0:T(8,128)(2,1)} %x_in.1, bf16[32,512]{1,0:T(8,128)(2,1)} %g_in.1, bf16[1848,512]{1,0:T(8,128)(2,1)} %bitcast.4, bf16[1848,512]{1,0:T(8,128)(2,1)} %bitcast.5, ...), custom_call_target="tpu_custom_call" | custom-call | flops 8719958016 | bytes 11354112 | tf_op jit(solution)/shard_map/pallas_call | solution.py:351
  83.6 2.8 %shard_map.85 = (bf16[32,512]{1,0:T(8,128)(2,1)}, bf16[1848,512]{1,0:T(8,128)(2,1)}, bf16[1848,512]{1,0:T(8,128)(2,1)}, bf16[1848,512]{1,0:T(8,128)(2,1)}) custom-call(bf16[32,512]{1,0:T(8,128)(2,1)S(1)} %get-tuple-element.12.refs_0_, bf16[1848,512]{1,0:T(8,128)(2,1)S(1)} %get-tuple-element.13.refs_1_, bf16[1848,512]{1,0:T(8,128)(2,1)S(1)} %get-tuple-element.14.refs_2_, ...), custom_call_target="tpu_custom_call" | custom-call | tf_op jit(solution)/shard_map/pallas_call | solution.py:402

commit v4 on v3

--- a/solution.py
+++ b/solution.py
@@ -12,10 +12,11 @@
 
 NEAR = [(0, 0), (0, 1), (1, 0), (1, 1), (-1, 0), (-1, 1), (2, 0), (-2, 0)]
 NEAR += [(2, 1), (-2, 1), (3, 0), (3, 1), (-3, 0), (-3, 1), (4, 0), (4, 1)]
+FAR = (6, 2, 4)
 CHUNK = 640
 UNITS = [(g, k) for g in range(2) for k in range(3)]
-SUM_Y_FIRST = (True, False, True, False, False, True)
-SPREAD_X_FIRST = (True, True, False, False, True, True)
+SUM_Y_FIRST = (True, False, True, False, True, True)
+SPREAD_X_FIRST = (True, True, True, False, False, True)
 
 
 def contract(left, right, left_dim, right_dim):
@@ -40,9 +41,9 @@
     x_in, g_in, wg_in, wu_in, wd_in,
     gi_out, gg_out, gu_out, gd_out,
     wg, wu, wd, x_all, g_all, part, pair, terms, got, mid, cross, got_cross,
-    acts, gi_acc, gi_send, gi_got, gg, gu, gd, gi,
+    acts, gi_acc, gi_send, gi_got, gi_lean, gg, gu, gd, gi,
     w_sem, near_send, near_recv, pair_send, pair_recv, sum_send, cross_send, sum_recv,
-    act_send, act_recv, half_send, half_recv, gi_ssem, gi_rsem, out_sem,
+    act_send, act_recv, half_send, half_recv, gi_ssem, gi_rsem, lean_sem, out_sem,
 ):
     row, col = lax.axis_index("row"), lax.axis_index("col")
     y, h, c = row // 4, (row // 2) % 2, row % 2
@@ -83,7 +84,7 @@
 
     with jax.named_scope("greet"):
       barrier = pltpu.get_barrier_semaphore()
-    peers = [partner, across] + [owner_at(dy, 0) for dy in (1, 2, 3)]
+    peers = [partner, across] + [owner_at(dy, 0) for dy in (1, 3)]
     peers += [near_at(*step) for step in NEAR[1:8]]
     for peer in peers:
         pl.semaphore_signal(barrier, inc=1, device_id=peer, device_id_type=MESH)
@@ -156,29 +157,33 @@
         weights_in(4)
         multiply(u, 2, g_all, wd)
 
+    def pass_to(u, src, slot, sem, dy):
+        remote(src, slot, sum_send.at[u], sum_recv.at[u, sem], owner_at(dy, 0)).start()
+
+    def own(u, a, hh, dy):
+        return part[u, a, c, hh, along(dy)] + pair[u, a, hh, along(dy)]
+
     def sum_first(u):
         settle(pair.at[u], pair_recv.at[u])
-        for a in range(3):
-            if SUM_Y_FIRST[u]:
+        if SUM_Y_FIRST[u]:
+            for a in range(3):
                 terms[u, :, :, a] = (part[u, a, c] + pair[u, a]).astype(BF16)
-            else:
+            pass_to(u, terms.at[u, 0, along(2)], got.at[u, 4], 2, 1)
+            pass_to(u, terms.at[u, 1, along(2)], got.at[u, 5], 3, 3)
+            pass_to(u, terms.at[u, 1, along(1)], got.at[u, 1], 0, 1)
+            pass_to(u, terms.at[u, 0, along(3)], got.at[u, 2], 0, 3)
+        else:
+            for a in range(3):
                 terms[u, 1 - h, :, a] = (part[u, a, c, 1 - h] + pair[u, a, 1 - h]).astype(BF16)
-        if SUM_Y_FIRST[u]:
-            for dy in (2, 1, 3):
-                remote(
-                    terms.at[u, :, along(dy)], got.at[u, 2 * dy - 2 : 2 * dy],
-                    sum_send.at[u], sum_recv.at[u, 0], owner_at(dy, 0),
-                ).start()
-        else:
             remote(terms.at[u, 1 - h], got.at[u, :4], sum_send.at[u], sum_recv.at[u, 0], across).start()
 
     def sum_second(u):
         if SUM_Y_FIRST[u]:
-            settle(got.at[u, :6], sum_recv.at[u, 0])
+            settle(got.at[u, :4], sum_recv.at[u, 0])
             n = sum(SUM_Y_FIRST[:u])
             for a in range(3):
-                total = part[u, a, c, 1 - h, y] + pair[u, a, 1 - h, y]
-                for i in range(3):
+                total = own(u, a, 1 - h, 0)
+                for i in range(2):
                     total = total + got[u, 2 * i + 1 - h, a].astype(F32)
                 cross[n, a] = total
             remote(cross.at[n], got_cross.at[n], cross_send.at[0], sum_recv.at[u, 1], across).start()
@@ -187,10 +192,29 @@
             for a in range(3):
                 total = part[u, a, c, h] + pair[u, a, h] + got[u, :4, a].astype(F32)
                 mid[u, :, a] = total.astype(BF16)
-            for dy in (2, 1, 3):
-                remote(
-                    mid.at[u, along(dy)], got.at[u, 3 + dy], sum_send.at[u], sum_recv.at[u, 1], owner_at(dy, 0)
-                ).start()
+            pass_to(u, mid.at[u, along(2), 0:2], got.at[u, 6, 0:2], 2, 1)
+            pass_to(u, mid.at[u, along(2), 2:3], got.at[u, 6, 2:3], 3, 3)
+            pass_to(u, mid.at[u, along(1), 2:3], got.at[u, 4, 2:3], 1, 1)
+            pass_to(u, mid.at[u, along(3), 0:2], got.at[u, 5, 0:2], 1, 3)
+
+    def sum_mid(u):
+        for dy in (1, 3):
+            if SUM_Y_FIRST[u]:
+                slot = 4 if dy == 1 else 5
+                hh = 0 if dy == 1 else 1
+                settle(got.at[u, slot], sum_recv.at[u, 2 if dy == 1 else 3])
+                for a in range(3):
+                    terms[u, hh, along(dy), a] = (own(u, a, hh, dy) + got[u, slot, a].astype(F32)).astype(BF16)
+                pass_to(u, terms.at[u, hh, along(dy)], got.at[u, 0 if dy == 1 else 3], 0, dy)
+            else:
+                first, last = (0, 2) if dy == 1 else (2, 3)
+                settle(got.at[u, 6, first:last], sum_recv.at[u, 2 if dy == 1 else 3])
+                for a in range(first, last):
+                    total = own(u, a, h, dy) + got[u, along(dy), a].astype(F32) + got[u, 6, a].astype(F32)
+                    mid[u, along(dy), a] = total.astype(BF16)
+                pass_to(
+                    u, mid.at[u, along(dy), first:last], got.at[u, 4 if dy == 1 else 5, first:last], 1, dy
+                )
 
     def block(u, dy, dh, arrays=slice(0, 3)):
         return acts.at[u, arrays, c, (h + dh) % 2, along(dy)]
@@ -204,29 +228,29 @@
         if SUM_Y_FIRST[u]:
             settle(got_cross.at[n], sum_recv.at[u, 1])
         else:
-            settle(got.at[u, 4:7], sum_recv.at[u, 1])
+            settle(got.at[u, 4:6], sum_recv.at[u, 1])
         for a in range(3):
-            total = part[u, a, c, h, y] + pair[u, a, h, y]
+            total = own(u, a, h, 0)
             if SUM_Y_FIRST[u]:
-                for i in range(3):
+                for i in range(2):
                     total = total + got[u, 2 * i + h, a].astype(F32)
                 total = total + got_cross[n, a]
             else:
                 total = total + got[u, y, a].astype(F32)
-                for i in range(3):
+                for i in range(2):
                     total = total + got[u, 4 + i, a].astype(F32)
             totals.append(total)
         for a, value in enumerate(pointwise(*totals)):
             acts[u, a, c, h, y] = value
-        own = block(u, 0, 0)
+        mine = block(u, 0, 0)
         if SPREAD_X_FIRST[u]:
-            spread(u, 0, own, across)
-            spread(u, 1, own, owner_at(1, 0))
-            spread(u, 3, own, owner_at(3, 0))
-        else:
-            spread(u, 0, own, owner_at(1, 0))
-            spread(u, 1, own, owner_at(3, 0))
-            spread(u, 3, own, across)
+            spread(u, 0, mine, across)
+            spread(u, 1, mine, owner_at(1, 0))
+            spread(u, 3, mine, owner_at(3, 0))
+        else:
+            spread(u, 0, mine, owner_at(1, 0))
+            spread(u, 1, mine, owner_at(3, 0))
+            spread(u, 3, mine, across)
 
     def spread_a(u):
         settle(block(u, 0, 0), act_recv.at[u, 0])
@@ -273,10 +297,23 @@
         summed[g] += 1
         if summed[g] == 3:
             gi_send[g] = term.astype(BF16).reshape(8, 32, 512)
-            for b in reversed(range(8)):
-                i = g * 8 + b
-                if i:
-                    remote(gi_send.at[g, b], gi_got.at[i], gi_ssem.at[0], gi_rsem.at[0], near_at(*NEAR[i])).start()
+            if g == 1:
+                for j, b in enumerate(FAR):
+                    remote(
+                        gi_send.at[1, b + 1], gi_lean.at[j], gi_ssem.at[0], lean_sem.at[j], near_at(0, 1)
+                    ).start()
+            for b in reversed(range(1, 8)) if g == 0 else range(2):
+                give(g, b)
+
+    def give(g, b):
+        i = g * 8 + b
+        remote(gi_send.at[g, b], gi_got.at[i], gi_ssem.at[0], gi_rsem.at[0], near_at(*NEAR[i])).start()
+
+    def gi_pass(j):
+        b = FAR[j]
+        settle(gi_lean.at[j], lean_sem.at[j])
+        gi_send[1, b] = (gi_acc[1, 32 * b : 32 * b + 32] + gi_lean[j].astype(F32)).astype(BF16)
+        give(1, b)
 
     def weight_grads(k):
         rows = slice(k * CHUNK, k * CHUNK + width(k))
@@ -286,25 +323,27 @@
 
     plan = [
         (gather_near, 0), (gather_near, 1),
-        (gather, 1, 1, 0), (gate_up, 0), (gather, 2, 0, 0), (gate_up, 1),
-        (gather, 1, 1, 1), (back, 0), (gather, 2, 0, 1), (back, 1),
-        (gather, 2, 1, 0), (gather, 3, 0, 0), (gate_up, 2), (back, 2),
-        (gather, 2, 1, 1), (gather, 3, 0, 1), (sum_first, 0), (sum_first, 1),
-        (gather, 3, 1, 0), (gather, 3, 1, 1), (sum_first, 2), (gate_up, 3),
-        (gate_up, 5), (gate_up, 4), (sum_second, 0), (back, 3),
-        (back, 5), (sum_second, 1), (back, 4), (sum_first, 3),
-        (sum_first, 5), (sum_first, 4), (sum_second, 2), (reduce, 0),
-        (reduce, 1), (sum_second, 3), (sum_second, 5), (sum_second, 4),
-        (reduce, 2), (reduce, 3), (spread_a, 0), (spread_b, 0),
-        (spread_a, 1), (spread_b, 1), (reduce, 4), (spread_a, 2),
-        (spread_b, 2), (reduce, 5), (spread_a, 3), (spread_b, 3),
-        (spread_c, 0), (spread_c, 1), (spread_a, 4), (spread_b, 4),
-        (spread_c, 2), (spread_c, 3), (spread_a, 5), (spread_b, 5),
-        (spread_last, 0), (spread_last, 1), (input_grad, 0), (spread_c, 4),
-        (input_grad, 1), (spread_last, 2), (spread_c, 5), (spread_last, 3),
-        (input_grad, 2), (spread_last, 4), (input_grad, 3), (spread_last, 5),
-        (weight_grads, 0), (input_grad, 4), (input_grad, 5), (weight_grads, 2),
-        (weight_grads, 1),
+        (gather, 1, 1, 0), (gate_up, 2), (gather, 2, 0, 0), (gate_up, 1),
+        (gather, 1, 1, 1), (back, 2), (gather, 2, 0, 1), (back, 1),
+        (gather, 2, 1, 0), (gather, 3, 0, 0), (gate_up, 0), (back, 0),
+        (gather, 2, 1, 1), (gather, 3, 0, 1), (sum_first, 2), (sum_first, 1),
+        (gather, 3, 1, 0), (gather, 3, 1, 1), (sum_first, 0), (sum_mid, 2),
+        (gate_up, 4), (gate_up, 3), (back, 4), (back, 3),
+        (sum_mid, 0), (gate_up, 5), (sum_second, 2), (sum_first, 4),
+        (sum_second, 1), (sum_first, 3), (back, 5), (sum_second, 0),
+        (sum_first, 5), (sum_mid, 4), (reduce, 2), (sum_mid, 1),
+        (sum_mid, 5), (sum_second, 4), (sum_second, 3), (reduce, 1),
+        (reduce, 0), (sum_second, 5), (spread_a, 2), (sum_mid, 3),
+        (spread_b, 2), (reduce, 4), (spread_a, 1), (spread_b, 1),
+        (spread_c, 2), (reduce, 3), (spread_a, 0), (spread_b, 0),
+        (spread_a, 4), (spread_b, 4), (reduce, 5), (spread_c, 1),
+        (spread_last, 2), (spread_a, 3), (spread_b, 3), (input_grad, 2),
+        (spread_c, 0), (spread_c, 4), (spread_a, 5), (spread_b, 5),
+        (spread_last, 1), (spread_c, 3), (spread_last, 0), (input_grad, 1),
+        (spread_c, 5), (spread_last, 4), (input_grad, 0), (spread_last, 3),
+        (input_grad, 4), (spread_last, 5), (weight_grads, 1), (input_grad, 3),
+        (input_grad, 5), (weight_grads, 2), (weight_grads, 0), (gi_pass, 0),
+        (gi_pass, 1), (gi_pass, 2),
     ]
     for stage, *at in plan:
         stage(*at)
@@ -314,9 +353,9 @@
     ]
     for out in outs[:3]:
         out.start()
-    settle(gi_got.at[1:16], gi_rsem.at[0])
+    settle(gi_got.at[:12], gi_rsem.at[0])
     total = gi_acc[0, :32]
-    for i in range(1, 16):
+    for i in [*range(1, 10), *(8 + b for b in FAR)]:
         total = total + gi_got[i].astype(F32)
     gi[...] = total.astype(BF16)
     outs[3].start()
@@ -370,6 +409,7 @@
             vmem((2, 256, depth), F32),
             vmem((2, 8, rows, depth), BF16),
             vmem((16, rows, depth), BF16),
+            vmem((3, rows, depth), BF16),
             vmem((ff, depth), BF16),
             vmem((ff, depth), BF16),
             vmem((ff, depth), BF16),
@@ -381,13 +421,14 @@
             dma((units,)),
             dma((units,)),
             dma((1,)),
-            dma((units, 2)),
+            dma((units, 4)),
             dma((units,)),
             dma((units, 4)),
             dma((1,)),
             dma((units,)),
             dma((1,)),
             dma((1,)),
+            dma((3,)),
             dma((4,)),
         ],
         compiler_params=pltpu.CompilerParams(

time: 87.5 us -> 84.5 us (0.966); the launches traced: 86.4 us -> 84.4 us
  Pallas kernels: 85.8 us -> 83.8 us
    pallas_call x1, Pallas kernels: 83 us -> 81 us  [on_device(): pl.pallas_call(kernel, out_shape=results, in_specs=[anywhere] * 5, out_sp...]
where the time goes in v4:
time: 84.5 us; the launch traced here: 84.4 us
  Pallas kernels  83.8 us (99%)
    pallas_call x1, Pallas kernels, on_device(): pl.pallas_call(kernel, out_shape=results, in_specs=[anywhere] * 5, out_sp...  81 us
    pallas_call x1, Pallas kernels, on_device(): pl.pallas_call(place, grid=(pl.cdiv(ff, 616),), out_shape=results, in_spe...  2.76 us

profile of v4, /device:TPU:2, one launch (start us, length us, event | category | flops | bytes accessed | tf_op | source)
XLA Modules:
  0.0 84.4 jit_solution(14083288255306866550)
XLA Ops:
  0.6 81.0 %shard_map.84 = (bf16[32,512]{1,0:T(8,128)(2,1)S(1)}, bf16[1848,512]{1,0:T(8,128)(2,1)S(1)}, bf16[1848,512]{1,0:T(8,128)(2,1)S(1)}, bf16[1848,512]{1,0:T(8,128)(2,1)S(1)}) custom-call(bf16[32,512]{1,0:T(8,128)(2,1)} %x_in.1, bf16[32,512]{1,0:T(8,128)(2,1)} %g_in.1, bf16[1848,512]{1,0:T(8,128)(2,1)} %bitcast.4, bf16[1848,512]{1,0:T(8,128)(2,1)} %bitcast.5, ...), custom_call_target="tpu_custom_call" | custom-call | flops 8719958016 | bytes 11354112 | tf_op jit(solution)/shard_map/pallas_call | solution.py:390
  81.7 2.8 %shard_map.85 = (bf16[32,512]{1,0:T(8,128)(2,1)}, bf16[1848,512]{1,0:T(8,128)(2,1)}, bf16[1848,512]{1,0:T(8,128)(2,1)}, bf16[1848,512]{1,0:T(8,128)(2,1)}) custom-call(bf16[32,512]{1,0:T(8,128)(2,1)S(1)} %get-tuple-element.12.refs_0_, bf16[1848,512]{1,0:T(8,128)(2,1)S(1)} %get-tuple-element.13.refs_1_, bf16[1848,512]{1,0:T(8,128)(2,1)S(1)} %get-tuple-element.14.refs_2_, ...), custom_call_target="tpu_custom_call" | custom-call | tf_op jit(solution)/shard_map/pallas_call | solution.py:443

commit v5 on v4

--- a/solution.py
+++ b/solution.py
@@ -15,8 +15,8 @@
 FAR = (6, 2, 4)
 CHUNK = 640
 UNITS = [(g, k) for g in range(2) for k in range(3)]
-SUM_Y_FIRST = (True, False, True, False, True, True)
-SPREAD_X_FIRST = (True, True, True, False, False, True)
+SUM_Y_FIRST = (False, True, True, True, False, True)
+SPREAD_X_FIRST = (True, True, False, False, True, True)
 
 
 def contract(left, right, left_dim, right_dim):
@@ -323,26 +323,26 @@
 
     plan = [
         (gather_near, 0), (gather_near, 1),
-        (gather, 1, 1, 0), (gate_up, 2), (gather, 2, 0, 0), (gate_up, 1),
-        (gather, 1, 1, 1), (back, 2), (gather, 2, 0, 1), (back, 1),
-        (gather, 2, 1, 0), (gather, 3, 0, 0), (gate_up, 0), (back, 0),
-        (gather, 2, 1, 1), (gather, 3, 0, 1), (sum_first, 2), (sum_first, 1),
-        (gather, 3, 1, 0), (gather, 3, 1, 1), (sum_first, 0), (sum_mid, 2),
-        (gate_up, 4), (gate_up, 3), (back, 4), (back, 3),
-        (sum_mid, 0), (gate_up, 5), (sum_second, 2), (sum_first, 4),
-        (sum_second, 1), (sum_first, 3), (back, 5), (sum_second, 0),
-        (sum_first, 5), (sum_mid, 4), (reduce, 2), (sum_mid, 1),
-        (sum_mid, 5), (sum_second, 4), (sum_second, 3), (reduce, 1),
-        (reduce, 0), (sum_second, 5), (spread_a, 2), (sum_mid, 3),
-        (spread_b, 2), (reduce, 4), (spread_a, 1), (spread_b, 1),
-        (spread_c, 2), (reduce, 3), (spread_a, 0), (spread_b, 0),
-        (spread_a, 4), (spread_b, 4), (reduce, 5), (spread_c, 1),
-        (spread_last, 2), (spread_a, 3), (spread_b, 3), (input_grad, 2),
-        (spread_c, 0), (spread_c, 4), (spread_a, 5), (spread_b, 5),
-        (spread_last, 1), (spread_c, 3), (spread_last, 0), (input_grad, 1),
-        (spread_c, 5), (spread_last, 4), (input_grad, 0), (spread_last, 3),
-        (input_grad, 4), (spread_last, 5), (weight_grads, 1), (input_grad, 3),
-        (input_grad, 5), (weight_grads, 2), (weight_grads, 0), (gi_pass, 0),
+        (gather, 1, 1, 0), (gate_up, 0), (gather, 2, 0, 0), (gate_up, 1),
+        (gather, 1, 1, 1), (back, 0), (gather, 2, 0, 1), (back, 1),
+        (gather, 2, 1, 0), (gather, 3, 0, 0), (sum_first, 0), (sum_first, 1),
+        (gather, 2, 1, 1), (gate_up, 2), (gather, 3, 1, 0), (gather, 3, 0, 1),
+        (back, 2), (gather, 3, 1, 1), (sum_mid, 1), (sum_first, 2),
+        (gate_up, 3), (gate_up, 4), (back, 3), (gate_up, 5),
+        (sum_second, 0), (sum_second, 1), (back, 4), (back, 5),
+        (sum_first, 3), (sum_mid, 2), (sum_first, 4), (sum_mid, 0),
+        (sum_first, 5), (sum_mid, 3), (reduce, 1), (sum_second, 2),
+        (reduce, 0), (sum_mid, 5), (sum_second, 4), (spread_a, 1),
+        (sum_second, 3), (spread_b, 1), (reduce, 2), (spread_a, 0),
+        (spread_b, 0), (sum_second, 5), (sum_mid, 4), (reduce, 3),
+        (spread_c, 1), (spread_a, 2), (spread_b, 2), (spread_c, 0),
+        (reduce, 5), (reduce, 4), (spread_a, 3), (spread_b, 3),
+        (spread_last, 1), (spread_c, 2), (spread_last, 0), (input_grad, 1),
+        (spread_a, 5), (spread_b, 5), (input_grad, 0), (spread_a, 4),
+        (spread_b, 4), (spread_c, 3), (spread_c, 5), (spread_last, 2),
+        (spread_c, 4), (spread_last, 3), (input_grad, 2), (spread_last, 5),
+        (input_grad, 3), (spread_last, 4), (weight_grads, 0), (input_grad, 5),
+        (input_grad, 4), (weight_grads, 2), (weight_grads, 1), (gi_pass, 0),
         (gi_pass, 1), (gi_pass, 2),
     ]
     for stage, *at in plan:

time: 84.5 us -> 82.1 us (0.972)
  Pallas kernels: 83.8 us -> 81 us
    pallas_call x1, Pallas kernels: 81 us -> 78.3 us  [on_device(): pl.pallas_call(kernel, out_shape=results, in_specs=[anywhere] * 5, out_sp...]
where the time goes in v5:
time: 82.1 us; the launch traced here: 81.7 us
  Pallas kernels  81 us (99%)
    pallas_call x1, Pallas kernels, on_device(): pl.pallas_call(kernel, out_shape=results, in_specs=[anywhere] * 5, out_sp...  78.3 us
    pallas_call x1, Pallas kernels, on_device(): pl.pallas_call(place, grid=(pl.cdiv(ff, 616),), out_shape=results, in_spe...  2.76 us

profile of v5, /device:TPU:2, one launch (start us, length us, event | category | flops | bytes accessed | tf_op | source)
XLA Modules:
  0.0 81.7 jit_solution(10323902575157425167)
XLA Ops:
  0.6 78.3 %shard_map.84 = (bf16[32,512]{1,0:T(8,128)(2,1)S(1)}, bf16[1848,512]{1,0:T(8,128)(2,1)S(1)}, bf16[1848,512]{1,0:T(8,128)(2,1)S(1)}, bf16[1848,512]{1,0:T(8,128)(2,1)S(1)}) custom-call(bf16[32,512]{1,0:T(8,128)(2,1)} %x_in.1, bf16[32,512]{1,0:T(8,128)(2,1)} %g_in.1, bf16[1848,512]{1,0:T(8,128)(2,1)} %bitcast.4, bf16[1848,512]{1,0:T(8,128)(2,1)} %bitcast.5, ...), custom_call_target="tpu_custom_call" | custom-call | flops 8719958016 | bytes 11354112 | tf_op jit(solution)/shard_map/pallas_call | solution.py:390
  78.9 2.8 %shard_map.85 = (bf16[32,512]{1,0:T(8,128)(2,1)}, bf16[1848,512]{1,0:T(8,128)(2,1)}, bf16[1848,512]{1,0:T(8,128)(2,1)}, bf16[1848,512]{1,0:T(8,128)(2,1)}) custom-call(bf16[32,512]{1,0:T(8,128)(2,1)S(1)} %get-tuple-element.12.refs_0_, bf16[1848,512]{1,0:T(8,128)(2,1)S(1)} %get-tuple-element.13.refs_1_, bf16[1848,512]{1,0:T(8,128)(2,1)S(1)} %get-tuple-element.14.refs_2_, ...), custom_call_target="tpu_custom_call" | custom-call | tf_op jit(solution)/shard_map/pallas_call | solution.py:443

commit v6 on v5

--- a/solution.py
+++ b/solution.py
@@ -82,8 +82,7 @@
     for load in loads:
         load.start()
 
-    with jax.named_scope("greet"):
-      barrier = pltpu.get_barrier_semaphore()
+    barrier = pltpu.get_barrier_semaphore()
     peers = [partner, across] + [owner_at(dy, 0) for dy in (1, 3)]
     peers += [near_at(*step) for step in NEAR[1:8]]
     for peer in peers:
@@ -116,11 +115,13 @@
 
     def gather(far, dx, n):
         for way in (1, -1):
-            if far == 3 and (way == 1) == bool(dx):
+            if far == 3 and way == -1:
                 continue
             slot = slot_of(-way * far, dx)
             arrived(n, slot)
             hand(n, slot, near_at(way, 0), slot_of(-way * (far + 1) if far < 3 else 4, dx))
+            if (far, dx, way) == (2, 1, -1):
+                hand(n, slot, near_at(-2, 0), slot_of(4, 1))
 
     loaded = set()
 
@@ -143,7 +144,7 @@
             part[u, a, :, :, :, :, CHUNK - 128 :] = jnp.zeros((2, 2, 4, 16, 128), F32)
         product = contract(tokens(ref, g), weight[k * CHUNK : k * CHUNK + w, :], 1, 1)
         part[u, a, :, :, :, :, :w] = product.reshape(2, 2, 4, 16, w)
-        remote(part.at[u, a, 1 - c], pair.at[u, a], pair_send.at[0], pair_recv.at[u], partner).start()
+        remote(part.at[u, a, 1 - c], pair.at[u, a], pair_send.at[0], pair_recv.at[u, a // 2], partner).start()
 
     def gate_up(u):
         landed(0, UNITS[u][0])
@@ -163,19 +164,25 @@
     def own(u, a, hh, dy):
         return part[u, a, c, hh, along(dy)] + pair[u, a, hh, along(dy)]
 
-    def sum_first(u):
-        settle(pair.at[u], pair_recv.at[u])
+    def sum_first(u, start=0, stop=3):
+        span = slice(start, stop)
+        if start < 2:
+            settle(pair.at[u, :2], pair_recv.at[u, 0])
+        if stop == 3:
+            settle(pair.at[u, 2], pair_recv.at[u, 1])
         if SUM_Y_FIRST[u]:
-            for a in range(3):
+            for a in range(start, stop):
                 terms[u, :, :, a] = (part[u, a, c] + pair[u, a]).astype(BF16)
-            pass_to(u, terms.at[u, 0, along(2)], got.at[u, 4], 2, 1)
-            pass_to(u, terms.at[u, 1, along(2)], got.at[u, 5], 3, 3)
-            pass_to(u, terms.at[u, 1, along(1)], got.at[u, 1], 0, 1)
-            pass_to(u, terms.at[u, 0, along(3)], got.at[u, 2], 0, 3)
-        else:
-            for a in range(3):
+            pass_to(u, terms.at[u, 0, along(2), span], got.at[u, 4, span], 2, 1)
+            pass_to(u, terms.at[u, 1, along(2), span], got.at[u, 5, span], 3, 3)
+            pass_to(u, terms.at[u, 1, along(1), span], got.at[u, 1, span], 0, 1)
+            pass_to(u, terms.at[u, 0, along(3), span], got.at[u, 2, span], 0, 3)
+        else:
+            for a in range(start, stop):
                 terms[u, 1 - h, :, a] = (part[u, a, c, 1 - h] + pair[u, a, 1 - h]).astype(BF16)
-            remote(terms.at[u, 1 - h], got.at[u, :4], sum_send.at[u], sum_recv.at[u, 0], across).start()
+            remote(
+                terms.at[u, 1 - h, :, span], got.at[u, :4, span], sum_send.at[u], sum_recv.at[u, 0], across
+            ).start()
 
     def sum_second(u):
         if SUM_Y_FIRST[u]:
@@ -323,11 +330,12 @@
 
     plan = [
         (gather_near, 0), (gather_near, 1),
-        (gather, 1, 1, 0), (gate_up, 0), (gather, 2, 0, 0), (gate_up, 1),
-        (gather, 1, 1, 1), (back, 0), (gather, 2, 0, 1), (back, 1),
-        (gather, 2, 1, 0), (gather, 3, 0, 0), (sum_first, 0), (sum_first, 1),
-        (gather, 2, 1, 1), (gate_up, 2), (gather, 3, 1, 0), (gather, 3, 0, 1),
-        (back, 2), (gather, 3, 1, 1), (sum_mid, 1), (sum_first, 2),
+        (gather, 1, 1, 0), (gate_up, 1), (gather, 2, 0, 0), (gate_up, 0),
+        (gather, 1, 1, 1), (back, 1), (gather, 2, 0, 1), (sum_first, 1, 0, 2),
+        (back, 0), (gather, 2, 1, 0), (sum_first, 0, 0, 2), (sum_first, 1, 2, 3),
+        (gather, 3, 0, 0), (sum_first, 0, 2, 3),
+        (gate_up, 2), (gather, 2, 1, 1), (gather, 3, 0, 1), (back, 2),
+        (sum_mid, 1), (sum_first, 2),
         (gate_up, 3), (gate_up, 4), (back, 3), (gate_up, 5),
         (sum_second, 0), (sum_second, 1), (back, 4), (back, 5),
         (sum_first, 3), (sum_mid, 2), (sum_first, 4), (sum_mid, 0),
@@ -418,7 +426,7 @@
             dma((2,)),
             dma((2, 16)),
             dma((1,)),
-            dma((units,)),
+            dma((units, 2)),
             dma((units,)),
             dma((1,)),
             dma((units, 4)),

time: 82.1 us -> 81.7 us (level)
  no operation moved by 1% of the time
where the time goes in v6:
time: 81.7 us; the launch traced here: 81.6 us
  Pallas kernels  81 us (99%)
    pallas_call x1, Pallas kernels, on_device(): pl.pallas_call(kernel, out_shape=results, in_specs=[anywhere] * 5, out_sp...  78.2 us
    pallas_call x1, Pallas kernels, on_device(): pl.pallas_call(place, grid=(pl.cdiv(ff, 616),), out_shape=results, in_spe...  2.76 us

profile of v6, /device:TPU:2, one launch (start us, length us, event | category | flops | bytes accessed | tf_op | source)
XLA Modules:
  0.0 81.6 jit_solution(11329517797378918834)
XLA Ops:
  0.6 78.2 %shard_map.84 = (bf16[32,512]{1,0:T(8,128)(2,1)S(1)}, bf16[1848,512]{1,0:T(8,128)(2,1)S(1)}, bf16[1848,512]{1,0:T(8,128)(2,1)S(1)}, bf16[1848,512]{1,0:T(8,128)(2,1)S(1)}) custom-call(bf16[32,512]{1,0:T(8,128)(2,1)} %x_in.1, bf16[32,512]{1,0:T(8,128)(2,1)} %g_in.1, bf16[1848,512]{1,0:T(8,128)(2,1)} %bitcast.4, bf16[1848,512]{1,0:T(8,128)(2,1)} %bitcast.5, ...), custom_call_target="tpu_custom_call" | custom-call | flops 8719958016 | bytes 11354112 | tf_op jit(solution)/shard_map/pallas_call | solution.py:398
  78.8 2.8 %shard_map.85 = (bf16[32,512]{1,0:T(8,128)(2,1)}, bf16[1848,512]{1,0:T(8,128)(2,1)}, bf16[1848,512]{1,0:T(8,128)(2,1)}, bf16[1848,512]{1,0:T(8,128)(2,1)}) custom-call(bf16[32,512]{1,0:T(8,128)(2,1)S(1)} %get-tuple-element.12.refs_0_, bf16[1848,512]{1,0:T(8,128)(2,1)S(1)} %get-tuple-element.13.refs_1_, bf16[1848,512]{1,0:T(8,128)(2,1)S(1)} %get-tuple-element.14.refs_2_, ...), custom_call_target="tpu_custom_call" | custom-call | tf_op jit(solution)/shard_map/pallas_call | solution.py:451

commit v7 on v6

--- a/solution.py
+++ b/solution.py
@@ -335,7 +335,7 @@
         (back, 0), (gather, 2, 1, 0), (sum_first, 0, 0, 2), (sum_first, 1, 2, 3),
         (gather, 3, 0, 0), (sum_first, 0, 2, 3),
         (gate_up, 2), (gather, 2, 1, 1), (gather, 3, 0, 1), (back, 2),
-        (sum_mid, 1), (sum_first, 2),
+        (sum_first, 2, 0, 2), (sum_mid, 1), (sum_first, 2, 2, 3),
         (gate_up, 3), (gate_up, 4), (back, 3), (gate_up, 5),
         (sum_second, 0), (sum_second, 1), (back, 4), (back, 5),
         (sum_first, 3), (sum_mid, 2), (sum_first, 4), (sum_mid, 0),

time: 81.7 us -> 81.8 us (level); the launches traced: 81.6 us -> 80.3 us
  Pallas kernels: 81 us -> 79.7 us
    pallas_call x1, Pallas kernels: 78.2 us -> 76.9 us  [on_device(): pl.pallas_call(kernel, out_shape=results, in_specs=[anywhere] * 5, out_sp...]
where the time goes in v7:
time: 81.8 us; the launch traced here: 80.3 us
  Pallas kernels  79.7 us (97%)
    pallas_call x1, Pallas kernels, on_device(): pl.pallas_call(kernel, out_shape=results, in_specs=[anywhere] * 5, out_sp...  76.9 us
    pallas_call x1, Pallas kernels, on_device(): pl.pallas_call(place, grid=(pl.cdiv(ff, 616),), out_shape=results, in_spe...  2.76 us

profile of v7, /device:TPU:2, one launch (start us, length us, event | category | flops | bytes accessed | tf_op | source)
XLA Modules:
  0.0 80.3 jit_solution(17107071488525833970)
XLA Ops:
  0.6 76.9 %shard_map.84 = (bf16[32,512]{1,0:T(8,128)(2,1)S(1)}, bf16[1848,512]{1,0:T(8,128)(2,1)S(1)}, bf16[1848,512]{1,0:T(8,128)(2,1)S(1)}, bf16[1848,512]{1,0:T(8,128)(2,1)S(1)}) custom-call(bf16[32,512]{1,0:T(8,128)(2,1)} %x_in.1, bf16[32,512]{1,0:T(8,128)(2,1)} %g_in.1, bf16[1848,512]{1,0:T(8,128)(2,1)} %bitcast.4, bf16[1848,512]{1,0:T(8,128)(2,1)} %bitcast.5, ...), custom_call_target="tpu_custom_call" | custom-call | flops 8719958016 | bytes 11354112 | tf_op jit(solution)/shard_map/pallas_call | solution.py:398
  77.6 2.8 %shard_map.85 = (bf16[32,512]{1,0:T(8,128)(2,1)}, bf16[1848,512]{1,0:T(8,128)(2,1)}, bf16[1848,512]{1,0:T(8,128)(2,1)}, bf16[1848,512]{1,0:T(8,128)(2,1)}) custom-call(bf16[32,512]{1,0:T(8,128)(2,1)S(1)} %get-tuple-element.12.refs_0_, bf16[1848,512]{1,0:T(8,128)(2,1)S(1)} %get-tuple-element.13.refs_1_, bf16[1848,512]{1,0:T(8,128)(2,1)S(1)} %get-tuple-element.14.refs_2_, ...), custom_call_target="tpu_custom_call" | custom-call | tf_op jit(solution)/shard_map/pallas_call | solution.py:451
